TPU v7x, 32 devices: a whole 2x2x4 slice. The times are simulated.
32 devices in a mesh: groups: 2 (over y), dp: 8 (over z, x), tensor: 2 (over core).
Axes of the slice: x: 2, y: 2, z: 4, core: 2. Of those that a mesh axis runs over, the one named last changes fastest.
Arguments:
- hidden: bfloat16 [256, 28672], P(('groups', 'dp')), parts along dimension 0, may hold values from -6 to 6
- cotangent: bfloat16 [256, 4096], P(('groups', 'dp'), 'tensor'), parts along dimension 0, may hold values from -6 to 6
- lengths: int32 [16], P('groups'), parts along dimension 0, may hold values from 1 to 32, 128 in all
Outputs:
- fisher: float32 [57344, 4096], P(('groups', 'dp'), 'tensor'), parts along dimension 0
There are 2 independent parts, one for each index of `groups`. A program takes and returns all parts, laid end to end along the dimension named above; each array names one. Nothing has to cross between parts.
Inputs may be any that keep to these rules, and one draw needn't show every extreme that they name: The lengths sum to 128; the largest is exactly 32.
All inputs are finite; a program needn't handle non-finite values.
Results may differ from a plain program's by a relative error of at most 0.0003.
Values may be sent and summed in bfloat16 or wider, within the bound.
No kernel may reach another device: no remote copies, remote signals or barrier semaphores. Data moves between devices by JAX's collectives and lax.ppermute only.
A program may use at most 384 MiB of HBM per device.

v0:
```python
import jax
import jax.numpy as jnp
from jax import lax
from jax.sharding import PartitionSpec as P


def shards(hidden, cotangent, lengths):
    rows_h = lax.all_to_all(hidden, "dp", split_axis=1, concat_axis=0, tiled=True)
    rows_c = lax.all_gather(cotangent, "dp", axis=0, tiled=True)
    total = rows_c.shape[0]
    seqs = lengths.shape[0]
    longest = total // 4
    ends = jnp.cumsum(lengths)
    starts = ends - lengths
    weights = 1.0 / lengths.astype(jnp.float32)
    contract = (((0,), (0,)), ((), ()))
    fisher = jnp.zeros((rows_h.shape[1], rows_c.shape[1]), jnp.float32)
    for s in range(seqs):
        lower = jnp.minimum(starts[s], total - longest)
        piece_h = lax.dynamic_slice_in_dim(rows_h, lower, longest, 0)
        piece_c = lax.dynamic_slice_in_dim(rows_c, lower, longest, 0)
        places = lower + jnp.arange(longest, dtype=jnp.int32)
        keep = (places >= starts[s]) & (places < ends[s])
        piece_c = jnp.where(keep[:, None], piece_c, jnp.zeros_like(piece_c))
        grad = lax.dot_general(piece_h, piece_c, contract, preferred_element_type=jnp.float32)
        fisher = fisher + grad * grad * weights[s]
    return fisher / jnp.float32(seqs)


def solution(mesh):
    return jax.shard_map(
        shards,
        mesh=mesh,
        in_specs=(P(("groups", "dp"), None), P(("groups", "dp"), "tensor"), P("groups")),
        out_specs=P(("groups", "dp"), "tensor"),
        check_vma=False,
    )
```

profile of v0, /device:TPU:0, one launch (start us, length us, event | category | flops | bytes accessed | tf_op | source)
XLA Modules:
  0.0 221.7 jit_solution(8924676200642469835)
XLA Ops:
  0.0 2.2 copy.8
  2.2 7.3 %all-to-all-start = ((bf16[16,8,3584]{2,0,1:T(8,128)(2,1)}), bf16[16,8,3584]{2,0,1:T(8,128)(2,1)S(1)}, u32[]{:S(2)}, u32[]{:S(2)}) async-start(bf16[16,8,3584]{2,0,1:T(8,128)(2,1)} %bitcast.33), calls=%async_computation | async-start | bytes 1835008 | tf_op jit(solution)/shard_map/all_to_all | solution.py:8
  9.4 0.8 reduce-window.4
  10.2 0.7 bitcast_subtract_fusion
  10.9 0.7 fusion.64
  16.6 0.7 fusion.63
  17.3 1.2 compare_and_fusion.6
  18.5 1.3 compare_and_fusion.7
  19.8 1.2 compare_and_fusion.2
  21.0 1.3 compare_and_fusion.3
  22.3 1.1 compare_and_fusion.4
  23.4 1.3 compare_and_fusion.5
  24.7 1.2 compare_and_fusion.1
  25.9 1.3 compare_and_fusion
  27.2 0.7 convert_divide_fusion
  27.9 0.7 fusion.65
  28.6 32.1 %all_gather.3 = bf16[128,2048]{1,0:T(8,128)(2,1)S(1)} all-gather(bf16[16,2048]{1,0:T(8,128)(2,1)} %param.4), channel_id=1, replica_groups=mesh['groups'=2,'dp'=8,'tensor'=2] {'dp'}, dimensions={0}, use_global_device_ids=true | all-gather | bytes 589824 | tf_op jit(solution)/shard_map/all_gather | solution.py:9
  60.7 0.0 all-to-all-done
  60.7 11.7 %fusion.11 = f32[3584,2048]{1,0:T(8,128)} fusion(bf16[128,3584]{1,0:T(8,128)(2,1)S(1)} %bitcast.34, s32[]{:T(128)S(6)} %select_n.59, bf16[128,2048]{1,0:T(8,128)(2,1)S(1)} %all_gather.3, pred[32]{0:T(512)(128)(4,1)S(1)} %compare_and_fusion.6), kind=kOutput, calls=%fused_computation.13 | convolution fusion | flops 469827584 | bytes 29722112 | tf_op jit(solution)/shard_map/dot_general | solution.py:25
  72.4 11.6 %fusion.13 = f32[3584,2048]{1,0:T(8,128)} fusion(bf16[128,3584]{1,0:T(8,128)(2,1)S(1)} %bitcast.35, s32[]{:T(128)S(6)} %select_n.57, bf16[128,2048]{1,0:T(8,128)(2,1)S(1)} %all_gather.3, pred[32]{0:T(512)(128)(4,1)S(1)} %compare_and_fusion.7), kind=kOutput, calls=%fused_computation.15 | convolution fusion | flops 469827584 | bytes 29722112 | tf_op jit(solution)/shard_map/dot_general | solution.py:25
  84.0 11.7 %fusion.3 = f32[3584,2048]{1,0:T(8,128)} fusion(bf16[128,3584]{1,0:T(8,128)(2,1)S(1)} %bitcast.36, s32[]{:T(128)S(6)} %select_n.67, bf16[128,2048]{1,0:T(8,128)(2,1)S(1)} %all_gather.3, pred[32]{0:T(512)(128)(4,1)S(1)} %compare_and_fusion.2), kind=kOutput, calls=%fused_computation.5 | convolution fusion | flops 469827584 | bytes 29722112 | tf_op jit(solution)/shard_map/dot_general | solution.py:25
  95.6 11.6 %fusion.5 = f32[3584,2048]{1,0:T(8,128)} fusion(bf16[128,3584]{1,0:T(8,128)(2,1)S(1)} %bitcast.37, s32[]{:T(128)S(6)} %select_n.65, bf16[128,2048]{1,0:T(8,128)(2,1)S(1)} %all_gather.3, pred[32]{0:T(512)(128)(4,1)S(1)} %compare_and_fusion.3), kind=kOutput, calls=%fused_computation.7 | convolution fusion | flops 469827584 | bytes 29722112 | tf_op jit(solution)/shard_map/dot_general | solution.py:25
  107.2 11.6 %fusion.7 = f32[3584,2048]{1,0:T(8,128)} fusion(bf16[128,3584]{1,0:T(8,128)(2,1)S(1)} %bitcast.38, s32[]{:T(128)S(6)} %select_n.63, bf16[128,2048]{1,0:T(8,128)(2,1)S(1)} %all_gather.3, pred[32]{0:T(512)(128)(4,1)S(1)} %compare_and_fusion.4), kind=kOutput, calls=%fused_computation.9 | convolution fusion | flops 469827584 | bytes 29722112 | tf_op jit(solution)/shard_map/dot_general | solution.py:25
  118.9 11.6 %fusion.9 = f32[3584,2048]{1,0:T(8,128)} fusion(bf16[128,3584]{1,0:T(8,128)(2,1)S(1)} %bitcast.39, s32[]{:T(128)S(6)} %select_n.61, bf16[128,2048]{1,0:T(8,128)(2,1)S(1)} %all_gather.3, pred[32]{0:T(512)(128)(4,1)S(1)} %compare_and_fusion.5), kind=kOutput, calls=%fused_computation.11 | convolution fusion | flops 469827584 | bytes 29722112 | tf_op jit(solution)/shard_map/dot_general | solution.py:25
  130.4 12.4 %fusion.1 = f32[3584,2048]{1,0:T(8,128)} fusion(bf16[128,3584]{1,0:T(8,128)(2,1)S(1)} %bitcast.40, s32[]{:T(128)S(6)} %select_n.69, bf16[128,2048]{1,0:T(8,128)(2,1)S(1)} %all_gather.3, pred[32]{0:T(512)(128)(4,1)S(1)} %compare_and_fusion.1), kind=kOutput, calls=%fused_computation.3 | convolution fusion | flops 469827584 | bytes 29722112 | tf_op jit(solution)/shard_map/dot_general | solution.py:25
  142.9 78.9 %add_multiply_fusion = f32[3584,2048]{1,0:T(8,128)} fusion(f32[3584,2048]{1,0:T(8,128)} %fusion.1, f32[3584,2048]{1,0:T(8,128)} %fusion.3, f32[3584,2048]{1,0:T(8,128)} %fusion.5, f32[3584,2048]{1,0:T(8,128)} %fusion.7, f32[3584,2048]{1,0:T(8,128)} %fusion.9, f32[3584,2048]{1,0:T(8,128)} %fusion.11, f32[3584,2048]{1,0:T(8,128)} %fusion.13, f32[]{:T(128)} %bitcast.28, ...), kind=kOutput, calls=%fused_computation | convolution fusion | flops 645988352 | bytes 235243040 | tf_op jit(solution)/shard_map/dot_general | solution.py:25
Async XLA Ops:
  2.2 58.5 %all-to-all-start = ((bf16[16,8,3584]{2,0,1:T(8,128)(2,1)}), bf16[16,8,3584]{2,0,1:T(8,128)(2,1)S(1)}, u32[]{:S(2)}, u32[]{:S(2)}) async-start(bf16[16,8,3584]{2,0,1:T(8,128)(2,1)} %bitcast.33), calls=%async_computation | async-start | bytes 1835008 | tf_op jit(solution)/shard_map/all_to_all | solution.py:8
where the time goes:
time: 222 us
  matrix products  161 us (73%)
  blocking collectives  32.1 us (14%)
  other arithmetic  12 us (5%)
  starting transfers between devices  7.25 us (3%)
  between operations  5.1 us (2%)
  local copies, waits for them, and re-layouts  4.18 us (2%)
    dot_general x8, matrix products, shards(): lax.dot_general(piece_h, piece_c, contract, preferred_element_type=jnp.fl...  161 us
    all_gather x1, blocking collectives, shards(): rows_c = lax.all_gather(cotangent, 'dp', axis=0, tiled=True)  32.1 us
    and x8, other arithmetic, shards(): keep = (places >= starts[s]) & (places < ends[s])  9.89 us
    all_to_all x1, starting transfers between devices, shards(): lax.all_to_all(hidden, 'dp', split_axis=1, concat_axis=0, tiled=True)  7.25 us
  transfers between devices with their start and end apart: 1, of which 0 were waited for; matrix products, arithmetic and copies ran while one was open for 6% of the time, Pallas kernels for 0%

commit v1 on v0

v1 whole, which is shorter than its diff:
```python
import functools
import jax
import jax.numpy as jnp
from jax import lax
from jax.experimental import pallas as pl
from jax.experimental.pallas import tpu as pltpu
from jax.sharding import PartitionSpec as P

FIRST = (((0,), (0,)), ((), ()))
PLAIN = (((1,), (0,)), ((), ()))
VMEM = pltpu.CompilerParams(vmem_limit_bytes=20 << 20)


def pack_kernel(where_ref, h_ref, c_ref, out_ref):
    half_h = h_ref.shape[1]
    out_ref[0, :, :half_h] = h_ref[...]
    out_ref[0, :, half_h:] = c_ref[...]


def pack(where, hidden, cotangent, dp):
    rows = hidden.shape[0]
    half_h, half_c = hidden.shape[1] // dp // 2, cotangent.shape[1] // 2
    return pl.pallas_call(
        pack_kernel,
        grid_spec=pltpu.PrefetchScalarGridSpec(
            num_scalar_prefetch=1,
            grid=(dp,),
            in_specs=[
                pl.BlockSpec((rows, half_h), lambda d, where: (0, 2 * d + where[0])),
                pl.BlockSpec((rows, half_c), lambda d, where: (0, lax.rem(d, 2))),
            ],
            out_specs=pl.BlockSpec((1, rows, half_h + half_c), lambda d, where: (d, 0, 0)),
        ),
        out_shape=jax.ShapeDtypeStruct((dp, rows, half_h + half_c), hidden.dtype),
        compiler_params=VMEM,
        name="pack",
    )(where, hidden, cotangent)


def kernel(seqs, longest, tile, tiles, quarters, lengths_ref, where_ref, *refs):
    h_refs, c_refs, out_ref = refs[:2], refs[2:4], refs[-4]
    pick_ref, c2_ref, h_ref = refs[-3:]
    total = c_refs[0].shape[0]
    step = pl.program_id(0)

    @pl.when(step == 0)
    def _():
        row = lax.broadcasted_iota(jnp.int32, (longest, total), 0)
        token = lax.broadcasted_iota(jnp.int32, (longest, total), 1)
        start = jnp.int32(0)
        for s in range(seqs):
            length = lengths_ref[s]
            take = jnp.logical_and(token == start + row, row < length)
            pick_ref[pl.ds(s * longest, longest), :] = jnp.where(take, 1.0, 0.0).astype(jnp.bfloat16)
            start = start + length

    def prepare(c_ref):
        for s in range(seqs):
            pick = pick_ref[pl.ds(s * longest, longest), :]
            rows = lax.dot_general(pick, c_ref[...], PLAIN, preferred_element_type=jnp.float32)
            size = jnp.full((1, 1), seqs * lengths_ref[s], jnp.int32).astype(jnp.float32)
            rows = rows * lax.rsqrt(size)
            high = rows.astype(jnp.bfloat16)
            low = (rows - high.astype(jnp.float32)).astype(jnp.bfloat16)
            c2_ref[s, :longest, :] = high
            c2_ref[s, longest:, :] = low

    for q, (h, c, fresh) in enumerate(quarters):
        if fresh:
            pl.when(step == q * tiles)(functools.partial(prepare, c_refs[c]))

    for i in range(2):
        inside = [q for q, (h, _, _) in enumerate(quarters) if h == i]
        if inside:
            hit = functools.reduce(jnp.logical_or, [step // tiles == q for q in inside])

            @pl.when(hit)
            def _(i=i):
                at = pl.multiple_of(lax.rem(step, tiles) * tile, tile)
                rows = lax.dot_general(
                    pick_ref[...], h_refs[i][:, pl.ds(at, tile)], PLAIN, preferred_element_type=jnp.float32
                )
                h_ref[...] = rows.astype(jnp.bfloat16)

    fisher = None
    for s in range(seqs):
        rows = h_ref[pl.ds(s * longest, longest), :]
        rows = jnp.concatenate([rows, rows], axis=0)
        grad = lax.dot_general(rows, c2_ref[s], FIRST, preferred_element_type=jnp.float32)
        fisher = grad * grad if s == 0 else fisher + grad * grad
    out_ref[...] = fisher


def blocks(lengths, where, h, c, quarters, before):
    total, half_h = h[0].shape
    half_c = c[0].shape[1]
    seqs = lengths.shape[0]
    longest = total // 4
    tile = 256
    tiles = half_h // tile

    def where_out(step, lengths, where):
        q = step // tiles
        hs = sum((q == n) * h for n, (h, _, _) in enumerate(quarters))
        cs = sum((q == n) * c for n, (_, c, _) in enumerate(quarters))
        return (where[0] ^ hs) * tiles + lax.rem(step, tiles), where[1] ^ cs

    whole = lambda a: pl.BlockSpec(a.shape, lambda step, lengths, where: (0, 0))
    args = [*h, *c]
    specs = [whole(a) for a in args]
    aliases = {}
    if before is not None:
        aliases = {2 + len(args): 0}
        args.append(before)
        specs.append(pl.BlockSpec(memory_space=pl.ANY))
    return pl.pallas_call(
        functools.partial(kernel, seqs, longest, tile, tiles, quarters),
        grid_spec=pltpu.PrefetchScalarGridSpec(
            num_scalar_prefetch=2,
            grid=(len(quarters) * tiles,),
            in_specs=specs,
            out_specs=pl.BlockSpec((tile, half_c), where_out),
            scratch_shapes=[
                pltpu.VMEM((seqs * longest, total), jnp.bfloat16),
                pltpu.VMEM((seqs, 2 * longest, half_c), jnp.bfloat16),
                pltpu.VMEM((seqs * longest, tile), jnp.bfloat16),
            ],
        ),
        out_shape=jax.ShapeDtypeStruct((2 * half_h, 2 * half_c), jnp.float32),
        input_output_aliases=aliases,
        compiler_params=VMEM,
        cost_estimate=pl.CostEstimate(
            flops=len(quarters) * half_h * half_c * 2 * 256 * seqs,
            bytes_accessed=len(quarters) * half_h * half_c * 4,
            transcendentals=0,
        ),
        name=f"fisher_{len(quarters)}",
    )(lengths, where, *args)


def fisher_long(lengths, rows_h, rows_c):
    total = rows_c.shape[0]
    seqs = lengths.shape[0]
    longest = total // 4
    ends = jnp.cumsum(lengths)
    starts = ends - lengths
    weights = 1.0 / lengths.astype(jnp.float32)
    fisher = jnp.zeros((rows_h.shape[1], rows_c.shape[1]), jnp.float32)
    for s in range(seqs):
        lower = jnp.minimum(starts[s], total - longest)
        piece_h = lax.dynamic_slice_in_dim(rows_h, lower, longest, 0)
        piece_c = lax.dynamic_slice_in_dim(rows_c, lower, longest, 0)
        places = lower + jnp.arange(longest, dtype=jnp.int32)
        keep = (places >= starts[s]) & (places < ends[s])
        piece_c = jnp.where(keep[:, None], piece_c, jnp.zeros_like(piece_c))
        grad = lax.dot_general(piece_h, piece_c, FIRST, preferred_element_type=jnp.float32)
        fisher = fisher + grad * grad * weights[s]
    return fisher / jnp.float32(seqs)


def shards(dp, tensor, hidden, cotangent, lengths):
    half_h, half_c = hidden.shape[1] // dp // 2, cotangent.shape[1] // 2
    if tensor != 2 or dp % 2 or dp * hidden.shape[0] > 128 or half_h % 256 or half_c % 128:
        rows_h = lax.all_to_all(hidden, "dp", split_axis=1, concat_axis=0, tiled=True)
        rows_c = lax.all_gather(cotangent, "dp", axis=0, tiled=True)
        return fisher_long(lengths, rows_h, rows_c)
    where = jnp.stack([lax.axis_index("tensor"), lax.axis_index("dp") % 2]).astype(jnp.int32)
    sent = pack(where, hidden, cotangent, dp)
    mine = lax.all_to_all(sent, "dp", split_axis=0, concat_axis=0, tiled=True)
    mine = mine.reshape(-1, half_h + half_c)
    mine_h, mine_c = mine[:, :half_h], mine[:, half_h:]
    other_h = lax.ppermute(mine_h, "tensor", [(0, 1), (1, 0)])
    other_c = lax.ppermute(mine_c, "dp", [(i, i ^ 1) for i in range(dp)])
    out = blocks(lengths, where, [mine_h, mine_h], [mine_c, mine_c], ((0, 0, True),), None)
    rest = ((1, 0, True), (1, 1, True), (0, 1, False))
    return blocks(lengths, where, [mine_h, other_h], [mine_c, other_c], rest, out)


def solution(mesh):
    return jax.shard_map(
        functools.partial(shards, mesh.shape["dp"], mesh.shape["tensor"]),
        mesh=mesh,
        in_specs=(P(("groups", "dp"), None), P(("groups", "dp"), "tensor"), P("groups")),
        out_specs=P(("groups", "dp"), "tensor"),
        check_vma=False,
    )
```

time: 222 us -> 77.9 us (0.35)
  matrix products: 161 us -> 0 us
  Pallas kernels: 0 us -> 47.4 us
  other arithmetic: 12 us -> 0.07 us
  blocking collectives: 32.1 us -> 25.9 us
  starting transfers between devices: 7.25 us -> 1.42 us
  between operations: 5.1 us -> 0.03 us
    dot_general x8 -> x0, matrix products: 161 us -> none  [shards(): lax.dot_general(piece_h, piece_c, contract, preferred_element_type=jnp.fl...]
    pallas_call x0 -> x3, Pallas kernels: none -> 47.4 us  [the longest x2 46.5 us: blocks(): pl.pallas_call(functools.partial(kernel, seqs, longest, tile, tiles, quar...]
    all_gather x1 -> x0, blocking collectives: 32.1 us -> none  [shards(): rows_c = lax.all_gather(cotangent, 'dp', axis=0, tiled=True)]
    all_to_all x0 -> x1, blocking collectives: none -> 25.9 us  [shards(): mine = lax.all_to_all(sent, 'dp', split_axis=0, concat_axis=0, tiled=True)]
    and x8 -> x0, other arithmetic: 9.89 us -> none  [shards(): keep = (places >= starts[s]) & (places < ends[s])]
    all_to_all x1 -> x0, starting transfers between devices: 7.25 us -> none  [shards(): lax.all_to_all(hidden, 'dp', split_axis=1, concat_axis=0, tiled=True)]
    unnamed x0 -> x6, local copies, waits for them, and re-layouts: none -> 2.67 us
  transfers between devices with their start and end apart: 1 -> 2, of which waited for: 0 -> 0; matrix products, arithmetic and copies ran while one was open for 6% -> 0% of each run, Pallas kernels for 0% -> 16%
where the time goes in v1:
time: 77.9 us; the launch traced here: 77.6 us
  Pallas kernels  47.4 us (61%)
  blocking collectives  25.9 us (33%)
  local copies, waits for them, and re-layouts  2.72 us (3%)
  starting transfers between devices  1.42 us (2%)
    pallas_call x2, Pallas kernels, blocks(): pl.pallas_call(functools.partial(kernel, seqs, longest, tile, tiles, quar...  46.5 us
    all_to_all x1, blocking collectives, shards(): mine = lax.all_to_all(sent, 'dp', split_axis=0, concat_axis=0, tiled=True)  25.9 us
    unnamed x6, local copies, waits for them, and re-layouts  2.67 us
  transfers between devices with their start and end apart: 2, of which 0 were waited for; matrix products, arithmetic and copies ran while one was open for 0% of the time, Pallas kernels for 16%

profile of v1, /device:TPU:0, one launch (start us, length us, event | category | flops | bytes accessed | tf_op | source)
XLA Modules:
  0.0 77.6 jit_solution(17418742497274643744)
XLA Ops:
  0.0 0.1 pad_add_fusion.where_ref
  0.1 0.0 copy-start
  0.1 1.2 %copy-done = bf16[16,28672]{1,0:T(8,128)(2,1)S(1)} copy-done((bf16[16,28672]{1,0:T(8,128)(2,1)S(1)}, bf16[16,28672]{1,0:T(8,128)(2,1)}, u32[]{:S(2)}) %copy-start) | copy-done | bytes 917528
  1.3 0.0 copy-start.1
  1.3 0.8 %copy-done.1 = bf16[16,2048]{1,0:T(8,128)(2,1)S(1)} copy-done((bf16[16,2048]{1,0:T(8,128)(2,1)S(1)}, bf16[16,2048]{1,0:T(8,128)(2,1)}, u32[]{:S(2)}) %copy-start.1) | copy-done | bytes 65560
  2.1 0.9 %pack.1 = bf16[8,16,2816]{2,1,0:T(8,128)(2,1)S(1)} custom-call(s32[2]{0:T(128)S(1)} %pad_add_fusion.where_ref, bf16[16,28672]{1,0:T(8,128)(2,1)S(1)} %copy-done, bf16[16,2048]{1,0:T(8,128)(2,1)S(1)} %copy-done.1), custom_call_target="tpu_custom_call" | custom-call | tf_op jit(solution)/shard_map/pack/pallas_call | solution.py:23
  3.0 25.9 %all_to_all.5 = bf16[8,16,2816]{2,1,0:T(8,128)(2,1)S(1)} all-to-all(bf16[8,16,2816]{2,1,0:T(8,128)(2,1)S(1)} %pack.1), channel_id=1, replica_groups=mesh['groups'=2,'dp'=8,'tensor'=2] {'dp'}, dimensions={0} | all-to-all | bytes 1441792 | tf_op jit(solution)/shard_map/all_to_all | solution.py:169
  29.0 1.4 %collective-permute-start.1 = (bf16[128,1024]{1,0:T(8,128)(2,1)S(1)}, bf16[128,1024]{1,0:T(8,128)(2,1)S(1)}, u32[]{:S(2)}, u32[]{:S(2)}) collective-permute-start(bf16[128,1024]{1,0:T(8,128)(2,1)S(1)} %slice.9.refs_2_.refs_3_), channel_id=1, source_target_pairs={{0,2},{2,0},{4,6},{6,4},{8,10},{10,8},{12,14},{14,12},{1,3},{3,1},... | collective-permute-start | bytes 786440 | tf_op jit(solution)/shard_map/ppermute | solution.py:173
  30.4 0.0 collective-permute-start
  30.4 0.0 copy-start.2
  30.4 0.7 copy-done.2
  31.1 12.3 %fisher_1.1.refs_4_ = f32[3584,2048]{1,0:T(8,128)} custom-call(s32[8]{0:T(128)S(1)} %copy-done.2, s32[2]{0:T(128)S(1)} %pad_add_fusion.where_ref, bf16[128,1792]{1,0:T(8,128)(2,1)S(1)} %slice.8.refs_0_.refs_1_, bf16[128,1792]{1,0:T(8,128)(2,1)S(1)} %slice.8.refs_0_.refs_1_, bf16[128,1024]{1,0:T(8,128)(2,1)S(1)} %slice.9.refs_2_.refs_3_, ...), custom_call_target="tpu_custom_call" | custom-call | flops 7516192768 | bytes 7340032 | tf_op jit(solution)/shard_map/fisher_1/pallas_call | solution.py:116
  43.4 0.0 collective-permute-done.1.refs_3_
  43.4 0.0 collective-permute-done.refs_1_
  43.4 34.1 %fisher_3.1 = f32[3584,2048]{1,0:T(8,128)} custom-call(s32[8]{0:T(128)S(1)} %copy-done.2, s32[2]{0:T(128)S(1)} %pad_add_fusion.where_ref, bf16[128,1792]{1,0:T(8,128)(2,1)S(1)} %slice.8.refs_0_.refs_1_, bf16[128,1792]{1,0:T(8,128)(2,1)S(1)} %collective-permute-done.refs_1_, ...), custom_call_target="tpu_custom_call", output_to_operand_aliasing={{}: (6, {})} | custom-call | flops 22548578304 | bytes 22020096 | tf_op jit(solution)/shard_map/fisher_3/pallas_call | solution.py:116
  (2 shorter events, 0.0 us)
Async XLA Ops:
  0.1 1.2 %copy-start = (bf16[16,28672]{1,0:T(8,128)(2,1)S(1)}, bf16[16,28672]{1,0:T(8,128)(2,1)}, u32[]{:S(2)}) copy-start(bf16[16,28672]{1,0:T(8,128)(2,1)} %h_ref.1) | copy-start | bytes 2752516
  1.3 0.8 %copy-start.1 = (bf16[16,2048]{1,0:T(8,128)(2,1)S(1)}, bf16[16,2048]{1,0:T(8,128)(2,1)}, u32[]{:S(2)}) copy-start(bf16[16,2048]{1,0:T(8,128)(2,1)} %c_ref.1) | copy-start | bytes 196612
  29.0 14.4 %collective-permute-start.1 = (bf16[128,1024]{1,0:T(8,128)(2,1)S(1)}, bf16[128,1024]{1,0:T(8,128)(2,1)S(1)}, u32[]{:S(2)}, u32[]{:S(2)}) collective-permute-start(bf16[128,1024]{1,0:T(8,128)(2,1)S(1)} %slice.9.refs_2_.refs_3_), channel_id=1, source_target_pairs={{0,2},{2,0},{4,6},{6,4},{8,10},{10,8},{12,14},{14,12},{1,3},{3,1},... | collective-permute-start | bytes 786440 | tf_op jit(solution)/shard_map/ppermute | solution.py:173
  30.4 13.0 %collective-permute-start = (bf16[128,1792]{1,0:T(8,128)(2,1)S(1)}, bf16[128,1792]{1,0:T(8,128)(2,1)S(1)}, u32[]{:S(2)}, u32[]{:S(2)}) collective-permute-start(bf16[128,1792]{1,0:T(8,128)(2,1)S(1)} %slice.8.refs_0_.refs_1_), channel_id=1, source_target_pairs={{0,1},{1,0},{2,3},{3,2},{4,5},{5,4},{6,7},{7,6},{8,9},{9,8},{10,11... | collective-permute-start | bytes 1376264 | tf_op jit(solution)/shard_map/ppermute | solution.py:172
  30.4 0.7 copy-start.2
